TPU v7x, 256 devices: a whole 4x4x8 slice. The times are simulated.
256 devices in a mesh: rad: 4 (over y), ma: 64 (over x, z, core).
Axes of the slice: x: 4, y: 4, z: 8, core: 2. Of those that a mesh axis runs over, the one named last changes fastest.
Arguments:
- velocity: bfloat16 [4, 3, 2, 1024, 1536], P('rad', None, None, 'ma'), may hold values from -0.1875 to 0.1875
- test_fields: bfloat16 [4, 2, 3, 2, 1024, 1536], P('rad', None, None, None, 'ma'), may hold values from -0.1875 to 0.1875
- order_slots: int32 [1024], replicated, may hold values from 0 to 1023, as said below
Outputs:
- emf_out: bfloat16 [4, 2, 3, 2, 1024, 1536], P('rad', None, None, None, 'ma')
- emf_deriv: bfloat16 [4, 2, 3, 2, 1024, 1536], P('rad', None, None, None, 'ma')
Inputs may be any that keep to these rules, and one draw needn't show every extreme that they name: `order_slots`: every order from 0 to 1023 stands in exactly one slot, and slots 2i and 2i + 1 hold two orders that sum to 1023.
All inputs are finite; a program needn't handle non-finite values.
Results may differ from a plain program's by a relative error of at most 0.0064.
Values may be sent and summed in bfloat16 or wider, within the bound.
A program may use at most 128 MiB of HBM per device.

v0:
```python
import math

import jax
import jax.numpy as jnp
import numpy as np
from jax import lax
from jax.sharding import PartitionSpec as P

NPHI = 3072


def live_mask(orders, cycle_ids, total_orders, total_cycles):
    nearest = jnp.minimum(cycle_ids + 1, total_cycles - cycle_ids)
    return orders[:, None] * total_cycles <= 2 * total_orders * nearest[None, :]


def phase_table(orders, first_lon, lon_count, lon_total):
    longitudes = first_lon + jnp.arange(lon_count, dtype=jnp.int32)
    phase_int = orders[:, None] * longitudes[None, :] % lon_total
    angles = phase_int.astype(jnp.float32) * (2.0 * math.pi / lon_total)
    return jnp.stack([jnp.cos(angles), -jnp.sin(angles)]).astype(jnp.bfloat16)


def cheb_matrix(level_count):
    levels_at = np.arange(level_count)
    points = np.cos(np.pi * levels_at / (level_count - 1))
    weights = np.where((levels_at == 0) | (levels_at == level_count - 1), 2.0, 1.0) * np.where(
        levels_at % 2 == 0, 1.0, -1.0
    )
    identity = np.eye(level_count)
    spread = points[:, None] - points[None, :] + identity
    offdiag = weights[:, None] / weights[None, :] / spread * (1.0 - identity)
    matrix = offdiag - identity * offdiag.sum(axis=1)[:, None]
    return jnp.asarray(matrix / level_count, dtype=jnp.float32)


def radial_derivative(values):
    deriv_mat = cheb_matrix(values.shape[0])
    result = jnp.tensordot(
        deriv_mat, values.astype(jnp.float32), axes=1, precision=lax.Precision.HIGHEST
    )
    return result.astype(jnp.bfloat16)


def cycle_emf(vel_grid, tst_grid, order_slots, first_cycle, cycle_all):
    level_count = vel_grid.shape[0]
    cycle_count = vel_grid.shape[4]
    total_orders = order_slots.shape[0]
    lon_total = NPHI
    lon_block = 512
    vel_flat = jnp.moveaxis(vel_grid.reshape(level_count * 3, 2 * total_orders, cycle_count), 1, 0)
    vel_flat = vel_flat.reshape(2 * total_orders, level_count * 3 * cycle_count)
    tst_flat = jnp.moveaxis(tst_grid.reshape(level_count * 6, 2 * total_orders, cycle_count), 1, 0)
    tst_flat = tst_flat.reshape(2 * total_orders, level_count * 6 * cycle_count)
    spectrum = jnp.zeros((2 * total_orders, level_count * 6 * cycle_count), jnp.float32)
    for block_index in range(lon_total // lon_block):
        phases = phase_table(order_slots, block_index * lon_block, lon_block, lon_total)
        phase_rows = phases.reshape(2 * total_orders, lon_block)
        phase_cols = phase_rows.T
        vel_cycle = jnp.dot(phase_cols, vel_flat, preferred_element_type=jnp.float32)
        vel_cycle = vel_cycle.reshape(lon_block, level_count, 1, 3, cycle_count)
        tst_cycle = jnp.dot(phase_cols, tst_flat, preferred_element_type=jnp.float32)
        tst_cycle = tst_cycle.reshape(lon_block, level_count, 2, 3, cycle_count)
        comp_x = (
            vel_cycle[:, :, :, 1] * tst_cycle[:, :, :, 2]
            - vel_cycle[:, :, :, 2] * tst_cycle[:, :, :, 1]
        )
        comp_y = (
            vel_cycle[:, :, :, 2] * tst_cycle[:, :, :, 0]
            - vel_cycle[:, :, :, 0] * tst_cycle[:, :, :, 2]
        )
        comp_z = (
            vel_cycle[:, :, :, 0] * tst_cycle[:, :, :, 1]
            - vel_cycle[:, :, :, 1] * tst_cycle[:, :, :, 0]
        )
        emf_cycle = jnp.stack([comp_x, comp_y, comp_z], axis=3).astype(jnp.bfloat16)
        emf_cycle = emf_cycle.reshape(lon_block, level_count * 6 * cycle_count)
        spectrum = spectrum + jnp.dot(phase_rows, emf_cycle, preferred_element_type=jnp.float32)
    spectrum = spectrum.reshape(2, total_orders, level_count, 6, cycle_count)
    cycle_ids = first_cycle + jnp.arange(cycle_count, dtype=jnp.int32)
    live_map = live_mask(order_slots, cycle_ids, total_orders, cycle_all).astype(jnp.float32)
    spectrum = (spectrum * lon_total ** (-0.5) * live_map[None, :, None, None, :]).astype(
        jnp.bfloat16
    )
    spectrum = jnp.transpose(spectrum, (2, 3, 0, 1, 4))
    return spectrum.reshape(level_count, 2, 3, 2, total_orders, cycle_count)


def per_device(velocity, test_fields, order_slots):
    lev_dev = velocity.shape[0]
    slot_dev = velocity.shape[3]
    cycle_all = velocity.shape[4]
    ma_count = lax.axis_size("ma")
    own_orders = lax.dynamic_slice_in_dim(order_slots, lax.axis_index("ma") * slot_dev, slot_dev)
    live_own = live_mask(
        own_orders, jnp.arange(cycle_all, dtype=jnp.int32), order_slots.shape[0], cycle_all
    ).astype(jnp.bfloat16)
    vel_live = velocity * live_own
    tst_live = test_fields.reshape(lev_dev, 6, 2, slot_dev, cycle_all) * live_own
    vel_grid, tst_grid = (
        lax.all_to_all(vel_live, "ma", split_axis=4, concat_axis=3, tiled=True),
        lax.all_to_all(tst_live, "ma", split_axis=4, concat_axis=3, tiled=True),
    )
    first_cycle = lax.axis_index("ma") * (cycle_all // ma_count)
    emf_local = cycle_emf(vel_grid, tst_grid, order_slots, first_cycle, cycle_all)
    emf_back = lax.all_to_all(emf_local, "ma", split_axis=4, concat_axis=5, tiled=True)
    columns = lax.all_to_all(emf_back, "rad", split_axis=5, concat_axis=0, tiled=True)
    derived_cols = radial_derivative(columns)
    deriv_back = lax.all_to_all(derived_cols, "rad", split_axis=0, concat_axis=5, tiled=True)
    return (emf_back, deriv_back)


def solution(mesh):
    return jax.shard_map(
        per_device,
        mesh=mesh,
        in_specs=(P("rad", None, None, "ma", None), P("rad", None, None, None, "ma", None), P()),
        out_specs=(P("rad", None, None, None, "ma", None), P("rad", None, None, None, "ma", None)),
        check_vma=False,
    )
```

profile of v0, /device:TPU:6, one launch (start us, length us, event | category | flops | bytes accessed | tf_op | source)
XLA Modules:
  0.0 307.4 jit_solution(15153902820560575896)
XLA Ops:
  3.5 3.7 %copy.39 = bf16[1,3,2,16,1536]{3,1,2,0,4:T(4,128)(2,1)S(1)} copy(bf16[1,3,2,16,1536]{4,3,2,1,0:T(8,128)(2,1)} %broadcast_multiply_fusion.1) | data formatting | bytes 589824 | tf_op jit(solution)/shard_map/mul | solution.py:98
  10.7 12.2 %all-to-all-start = ((bf16[64,2,1152]{2,1,0:T(2,128)(2,1)}), bf16[64,2,1152]{2,1,0:T(2,128)(2,1)S(1)}, u32[]{:S(2)}, u32[]{:S(2)}) async-start(bf16[64,2,1152]{2,1,0:T(2,128)(2,1)} %reshape.1450), calls=%async_computation | async-start | bytes 589824 | tf_op jit(solution)/shard_map/all_to_all | solution.py:101
  22.9 11.1 %copy.42 = bf16[1,2,3,2,16,1536]{4,3,2,1,5,0:T(2,128)(2,1)} copy(bf16[1,2,3,2,16,1536]{5,4,3,2,1,0:T(8,128)(2,1)} %param.5) | data formatting | bytes 1179648 | tf_op args[1]
  34.0 7.2 %fusion.41 = bf16[1536,1,6,2,16]{4,3,2,1,0:T(2,128)(2,1)} fusion(bf16[1,6,2,16,1536]{3,2,1,0,4:T(2,128)(2,1)} %bitcast.221, bf16[16,1536]{0,1:T(8,128)(2,1)S(1)} %compare_convert_fusion), kind=kLoop, calls=%fused_computation.149 | loop fusion | flops 294912 | bytes 1228800
  41.2 52.4 %cosine_convert_fusion = (bf16[1,1024,512]{2,1,0:T(8,128)(2,1)S(1)}, bf16[1,1024,512]{2,1,0:T(8,128)(2,1)S(1)}, bf16[1,1024,512]{2,1,0:T(8,128)(2,1)S(1)}, bf16[...) fusion(s32[512]{0:T(512)S(1)} %iota_add_fusion.1, ...), kind=kLoop, calls=%fused_computation.34 | loop fusion | flops 37748736 | bytes 12597248 | tf_op jit(solution)/shard_map/convert.3
  100.0 14.3 %reshape.1448 = bf16[64,2,2304]{2,1,0:T(2,128)(2,1)} reshape(bf16[1536,1,6,2,16]{4,3,2,1,0:T(2,128)(2,1)} %fusion.41) | data formatting | bytes 1179648
  114.4 10.9 %all-to-all-start.1 = ((bf16[64,2,2304]{2,1,0:T(2,128)(2,1)}), bf16[64,2,2304]{2,1,0:T(2,128)(2,1)S(1)}, u32[]{:S(2)}, u32[]{:S(2)}) async-start(bf16[64,2,2304]{2,1,0:T(2,128)(2,1)} %reshape.1448), calls=%async_computation.1 | async-start | bytes 1179648 | tf_op jit(solution)/shard_map/all_to_all | solution.py:102
  125.3 4.1 %reshape.1451 = bf16[1536,1,2,3,16]{4,3,2,1,0:T(4,128)(2,1)} reshape(bf16[64,2,1152]{2,1,0:T(2,128)(2,1)S(1)} %all-to-all-done) | data formatting | bytes 589824
  129.3 5.2 %copy.73 = bf16[1,3,2,16,64,24]{3,4,2,5,1,0:T(8,128)(2,1)} copy(bf16[1,3,2,16,64,24]{3,1,2,5,4,0:T(4,128)(2,1)} %bitcast.233) | data formatting | bytes 589824 | tf_op jit(solution)/shard_map/all_to_all | solution.py:101
  134.6 5.0 %reshape.1426 = bf16[3,2048,24]{1,2,0:T(8,128)(2,1)S(1)} reshape(bf16[1,3,2,64,16,24]{4,3,2,5,1,0:T(8,128)(2,1)} %bitcast.234) | data formatting | bytes 589824 | tf_op jit(solution)/shard_map/reshape | solution.py:51
  148.4 4.6 %reshape.1449 = bf16[1536,1,6,2,16]{4,3,2,1,0:T(2,128)(2,1)} reshape(bf16[64,2,2304]{2,1,0:T(2,128)(2,1)S(1)} %all-to-all-done.1) | data formatting | bytes 1179648
  153.0 7.5 %copy.71 = bf16[1,6,2,16,64,24]{3,4,2,5,1,0:T(8,128)(2,1)} copy(bf16[1,6,2,16,64,24]{3,2,1,5,4,0:T(2,128)(2,1)} %bitcast.222) | data formatting | bytes 1179648 | tf_op jit(solution)/shard_map/all_to_all | solution.py:102
  160.5 9.0 %reshape.1430 = bf16[6,2048,24]{1,2,0:T(8,128)(2,1)S(1)} reshape(bf16[1,6,2,64,16,24]{4,3,2,5,1,0:T(8,128)(2,1)} %bitcast.223) | data formatting | bytes 1179648 | tf_op jit(solution)/shard_map/reshape | solution.py:53
  186.5 7.1 %copy.45 = bf16[1,6,2,1024,24]{4,2,1,3,0:T(2,128)(2,1)S(1)} copy(bf16[1,6,2,1024,24]{3,2,4,1,0:T(2,128)(2,1)} %fusion.31) | data formatting | bytes 1179648 | tf_op jit(solution)/shard_map/transpose | solution.py:85
  193.6 5.1 %reshape.1452 = bf16[64,2,2304]{2,1,0:T(2,128)(2,1)} reshape(bf16[1024,1,2,3,2,24]{5,4,3,2,1,0:T(2,128)(2,1)S(1)} %bitcast.229) | data formatting | bytes 1179648
  198.6 28.6 %all_to_all.84 = bf16[64,2,2304]{2,1,0:T(2,128)(2,1)} all-to-all(bf16[64,2,2304]{2,1,0:T(2,128)(2,1)} %reshape.1452), channel_id=1, replica_groups=mesh['rad'=4,'ma'=64] {'ma'}, dimensions={0} | all-to-all | bytes 1179648 | tf_op jit(solution)/shard_map/all_to_all | solution.py:106
  227.3 11.1 %reshape.1453 = bf16[1024,1,2,3,2,24]{5,4,3,2,1,0:T(2,128)(2,1)S(1)} reshape(bf16[64,2,2304]{2,1,0:T(2,128)(2,1)} %all_to_all.84) | data formatting | bytes 1179648
  242.0 5.2 %all_to_all.70 = bf16[1,2,3,2,16,1536]{5,4,3,2,1,0:T(8,128)(2,1)S(1)} reshape(bf16[1,2,3,2,16,64,24]{6,5,4,3,2,1,0:T(8,128)(2,1)} %bitcast.231) | data formatting | bytes 1179648 | tf_op jit(solution)/shard_map/all_to_all | solution.py:106
  247.3 8.3 %copy.48 = bf16[1,2,3,2,16,1536]{4,3,2,1,0,5:T(2,128)(2,1)} copy(bf16[1,2,3,2,16,1536]{5,4,3,2,1,0:T(8,128)(2,1)S(1)} %all_to_all.70) | data formatting | bytes 1179648 | tf_op jit(solution)/shard_map/all_to_all | solution.py:106
  255.6 6.2 %reshape.1454 = bf16[4,2,36864]{2,1,0:T(2,128)(2,1)S(1)} reshape(bf16[1536,1,2,3,2,16]{5,4,3,2,1,0:T(2,128)(2,1)} %bitcast.225) | data formatting | bytes 1179648
  261.8 15.3 %all_to_all.85 = bf16[4,2,36864]{2,1,0:T(2,128)(2,1)S(1)} all-to-all(bf16[4,2,36864]{2,1,0:T(2,128)(2,1)S(1)} %reshape.1454), channel_id=1, replica_groups=mesh['rad'=4,'ma'=64] {'rad'}, dimensions={0} | all-to-all | bytes 1179648 | tf_op jit(solution)/shard_map/all_to_all | solution.py:107
  277.1 4.4 %reshape.1455 = bf16[1536,1,2,3,2,16]{5,4,3,2,1,0:T(2,128)(2,1)} reshape(bf16[4,2,36864]{2,1,0:T(2,128)(2,1)S(1)} %all_to_all.85) | data formatting | bytes 1179648
  281.5 10.9 %copy.65 = bf16[1,2,3,2,16,4,384]{6,5,4,3,2,1,0:T(4,128)(2,1)S(1)} copy(bf16[1,2,3,2,16,4,384]{4,3,2,1,6,5,0:T(2,128)(2,1)} %bitcast.224) | data formatting | bytes 1179648 | tf_op jit(solution)/shard_map/all_to_all | solution.py:107
  293.6 12.7 %all_to_all.86 = bf16[4,2,3,2,16,384]{5,4,3,2,1,0:T(8,128)(2,1)S(1)} all-to-all(bf16[4,2,3,2,16,384]{5,4,3,2,1,0:T(8,128)(2,1)S(1)} %copy.50), channel_id=1, replica_groups=mesh['rad'=4,'ma'=64] {'rad'}, dimensions={0} | all-to-all | bytes 1179648 | tf_op jit(solution)/shard_map/all_to_all | solution.py:109
  (103 shorter events, 43.9 us)
Async XLA Ops:
  10.7 103.7 %all-to-all-start = ((bf16[64,2,1152]{2,1,0:T(2,128)(2,1)}), bf16[64,2,1152]{2,1,0:T(2,128)(2,1)S(1)}, u32[]{:S(2)}, u32[]{:S(2)}) async-start(bf16[64,2,1152]{2,1,0:T(2,128)(2,1)} %reshape.1450), calls=%async_computation | async-start | bytes 589824 | tf_op jit(solution)/shard_map/all_to_all | solution.py:101
  34.0 7.2 %copy-start.19 = (s32[1024]{0:T(1024)S(1)}, s32[1024]{0:T(1024)}, u32[]{:S(2)}) copy-start(s32[1024]{0:T(1024)} %param.6) | copy-start | bytes 12292
  114.4 33.9 %all-to-all-start.1 = ((bf16[64,2,2304]{2,1,0:T(2,128)(2,1)}), bf16[64,2,2304]{2,1,0:T(2,128)(2,1)S(1)}, u32[]{:S(2)}, u32[]{:S(2)}) async-start(bf16[64,2,2304]{2,1,0:T(2,128)(2,1)} %reshape.1448), calls=%async_computation.1 | async-start | bytes 1179648 | tf_op jit(solution)/shard_map/all_to_all | solution.py:102
  139.6 2.9 copy-start.1
  142.5 1.6 copy-start.7
  144.6 1.6 copy-start.5
  146.3 1.6 copy-start.3
  169.6 2.2 copy-start.2
  171.8 1.6 copy-start.8
  173.9 1.6 copy-start.4
  175.4 1.6 copy-start.6
  177.0 0.8 copy-start.16
  177.0 0.8 copy-start.17
  177.0 0.8 copy-start.18
  178.0 0.9 copy-start.13
  178.0 0.9 copy-start.14
  178.0 0.9 copy-start.15
  178.0 1.0 copy-start.10
  178.0 1.0 copy-start.11
  178.0 1.0 copy-start.12
  181.8 1.6 copy-start
  247.3 8.3 %copy-start.9 = (bf16[1,2,3,2,16,1536]{5,4,3,2,1,0:T(8,128)(2,1)}, bf16[1,2,3,2,16,1536]{5,4,3,2,1,0:T(8,128)(2,1)S(1)}, u32[]{:S(2)}) copy-start(bf16[1,2,3,2,16,1536]{5,4,3,2,1,0:T(8,128)(2,1)S(1)} %all_to_all.70) | copy-start | bytes 1769476
  281.5 10.9 %copy-start.20 = (f32[4,4,1,1,1,1]{1,0,5,4,3,2:T(4,128)S(1)}, f32[4,4,1,1,1,1]{1,0,5,4,3,2:T(4,128)}, u32[]{:S(2)}) copy-start(f32[4,4,1,1,1,1]{1,0,5,4,3,2:T(4,128)} %constant.67) | copy-start | bytes 196
where the time goes:
time: 313 us; the launch traced here: 307 us
  local copies, waits for them, and re-layouts  141 us (45%)
  other arithmetic  70.5 us (23%)
  blocking collectives  56.6 us (18%)
  starting transfers between devices  23 us (7%)
  matrix products  15.2 us (5%)
    unnamed x52, local copies, waits for them, and re-layouts  71 us
    another operation x7, other arithmetic  52.7 us
    all_to_all x1, blocking collectives, per_device(): lax.all_to_all(emf_local, 'ma', split_axis=4, concat_axis=5, tiled=True)  28.6 us
    all_to_all x3, local copies, waits for them, and re-layouts, per_device(): lax.all_to_all(emf_local, 'ma', split_axis=4, concat_axis=5, tiled=True)  17.2 us
    all_to_all x1, blocking collectives, per_device(): lax.all_to_all(emf_back, 'rad', split_axis=5, concat_axis=0, tiled=True)  15.3 us
    all_to_all x1, blocking collectives, per_device(): lax.all_to_all(derived_cols, 'rad', split_axis=0, concat_axis=5, tiled=True)  12.7 us
    all_to_all x1, starting transfers between devices, per_device(): lax.all_to_all(vel_live, 'ma', split_axis=4, concat_axis=3, tiled=True)  12.2 us
    all_to_all x1, local copies, waits for them, and re-layouts, per_device(): lax.all_to_all(emf_back, 'rad', split_axis=5, concat_axis=0, tiled=True)  10.9 us
  transfers between devices with their start and end apart: 2, of which 0 were waited for; matrix products, arithmetic and copies ran while one was open for 37% of the time, Pallas kernels for 0%

commit v1 on v0

v1 whole, which is shorter than its diff:
```python
import functools

import jax
import jax.numpy as jnp
import numpy as np
from jax import lax
from jax.experimental import pallas as pl
from jax.experimental.pallas import tpu as pltpu
from jax.sharding import PartitionSpec as P

MESH = pl.DeviceIdType.MESH
M = 1024
NTH = 1536
NPHI = 3072
HALF = NPHI // 2
NR = 4
NMA = 64
F32 = jnp.float32
BF16 = jnp.bfloat16
I32 = jnp.int32
PB = 256


def cheb_matrix(level_count):
    levels_at = np.arange(level_count)
    points = np.cos(np.pi * levels_at / (level_count - 1))
    weights = np.where((levels_at == 0) | (levels_at == level_count - 1), 2.0, 1.0) * np.where(
        levels_at % 2 == 0, 1.0, -1.0
    )
    identity = np.eye(level_count)
    spread = points[:, None] - points[None, :] + identity
    offdiag = weights[:, None] / weights[None, :] / spread * (1.0 - identity)
    matrix = offdiag - identity * offdiag.sum(axis=1)[:, None]
    return np.asarray(matrix / level_count, dtype=np.float32)


DERIV = cheb_matrix(NR)


def phase_tables():
    r = np.arange(M // 2)
    p = np.arange(HALF)
    tabs = []
    for m in (2 * r, M - 1 - 2 * r):
        q = (m[:, None] * p[None, :]) % NPHI
        ang = q.astype(np.float32) * np.float32(2.0 * np.pi / NPHI)
        tabs.append(np.concatenate([np.cos(ang), -np.sin(ang)], axis=0).astype(jnp.bfloat16))
    inv = np.stack(tabs)
    fwd = np.ascontiguousarray(np.swapaxes(inv, 1, 2))
    return fwd, inv


def expand_table():
    tab = np.zeros((3, 128, 256), np.float32)
    groups = []
    for f in range(2):
        for g, c in enumerate((1, 2, 0, 1)):
            groups.append((12 * (4 * f + g), c))
    b_first = 128 + 116
    for f in range(2):
        base = 3 + 3 * f
        for g, c in enumerate((2, 0, 1)):
            groups.append((128 + 12 * (4 * f + g), base + c))
        groups.append((b_first if f == 0 else 128 + 36, base + 1))
    for lane0, c in groups:
        for h in range(2):
            for v in range(6):
                lane = lane0 + h * 6 + v
                tab[0, c * 12 + h * 6 + v, lane] = 1
                tab[1, c * 12 + (1 - h) * 6 + v, lane] = 1
                tab[2, 108 + h * 9 + c, lane] = 1
    return np.concatenate(list(tab), axis=1).astype(jnp.bfloat16)


OUT_GROUPS = (0, 1, 2, 4, 5, 6)


def fold_table():
    tab = np.zeros((2, 128, 128), np.float32)
    for g, grp in enumerate(OUT_GROUPS):
        for h in range(2):
            for v in range(6):
                lane = grp * 12 + h * 6 + v
                tab[0, grp * 12 + (1 - h) * 6 + v, lane] = 1
                tab[1, lane, 96 + h * 6 + g] = 1
    return np.concatenate(list(tab), axis=0).astype(jnp.bfloat16)


def dot(a, b):
    return jnp.dot(a, b, preferred_element_type=F32)


def iota(shape, dim):
    return lax.broadcasted_iota(I32, shape, dim)


def onehot(cond):
    return jnp.where(cond, 1.0, 0.0).astype(BF16)


def cross(x):
    a, b = x[:, :128], x[:, 128:]
    return a * b - pltpu.roll(a, 116, 1) * pltpu.roll(b, 12, 1)


def kernel(
    vel_ref, tst_ref, own_ref, tgtc_ref, tgtr_ref, keyc_ref, keyr_ref, exp_ref, fold_ref, fwd_hbm, inv_hbm,
    emf_ref, der_ref,
    fwd_tab, inv_tab, packed, turned, sendbuf, recvbuf, perm, permt, rhs_e, rhs_o, summed, differ, pout,
    outbuf, backbuf, radbuf, dersend, derbuf, quse, qback, rows,
    tab_sem, f_send, f_recv, b_send, b_recv, y_send, y_recv, d_send, d_recv,
):
    me = lax.axis_index("ma")
    lev = lax.axis_index("rad")

    barrier = pltpu.get_barrier_semaphore()

    def greet(step, carry):
        pl.semaphore_signal(
            barrier, inc=1, device_id=(lev, lax.rem(me + step, NMA)), device_id_type=MESH
        )
        return carry

    lax.fori_loop(1, NMA, greet, 0)
    for step in range(1, NR):
        pl.semaphore_signal(barrier, inc=1, device_id=(lax.rem(lev + step, NR), me), device_id_type=MESH)

    tab_f = pltpu.make_async_copy(fwd_hbm, fwd_tab, tab_sem.at[0])
    tab_i = pltpu.make_async_copy(inv_hbm, inv_tab, tab_sem.at[1])
    tab_f.start()
    tab_i.start()

    quse[...] = onehot(tgtc_ref[0:192] == iota((192, 192), 1))
    qback[...] = onehot(tgtr_ref[:, 0:192] == iota((192, 192), 0))
    even = own_ref[...]
    odd = (M - 1) - even
    lane = iota((16, 128), 1)

    def masks(v):
        out = []
        for h in range(2):
            j = 128 * v + lane
            near = (j + 1) if h == 0 else (768 - j)
            out.append((even * NTH <= 2 * M * near, odd * NTH <= 2 * M * near))
        return out

    left = {}
    for w in range(3):
        halves = []
        for h in range(2):
            cols = slice(768 * h + 256 * w, 768 * h + 256 * w + 256)
            halves.append(
                (dot(quse[0:96, 0:96], vel_ref[:, cols]), dot(quse[...], tst_ref[:, cols]))
            )
        for vv in range(2):
            v = 2 * w + vv
            live = masks(v)
            for c in range(9):
                xe, xo = [], []
                for h in range(2):
                    src = halves[h][0] if c < 3 else halves[h][1]
                    row = 32 * (c if c < 3 else c - 3)
                    xe.append(src[row : row + 16, 128 * vv : 128 * vv + 128])
                    xo.append(src[row + 16 : row + 32, 128 * vv : 128 * vv + 128])
                for h in range(2):
                    spot = (c * 12 + h * 6 + v) * 16
                    packed[spot : spot + 16, :] = jnp.where(live[h][0], xe[h], xo[1 - h])
                    rest = jnp.where(live[h][1] & live[1 - h][0], xo[h], 0.0)
                    left[h, c] = rest if v == 0 else left[h, c] + rest
    for h in range(2):
        for c in range(9):
            spot = (108 + h * 9 + c) * 16
            packed[spot : spot + 16, :] = left[h, c]
    packed[126 * 16 : 128 * 16, :] = jnp.zeros((32, 128), F32)
    for row in range(16):
        turned[pl.ds(row, 128, stride=16), :] = packed[pl.ds(row, 128, stride=16), :].T
    sendbuf[...] = turned[...].astype(BF16).reshape(128, 16, 128)

    pl.semaphore_wait(barrier, NMA - 1 + NR - 1)

    def all_to_all(src, dst, ssem, rsem, u):
        def one(step, carry):
            to = lax.rem(me + step, NMA)
            pltpu.make_async_remote_copy(
                src_ref=src.at[u * NMA + to],
                dst_ref=dst.at[u * NMA + me],
                send_sem=ssem.at[u],
                recv_sem=rsem.at[u],
                device_id=(lev, to),
                device_id_type=MESH,
            ).start()
            return carry

        pltpu.make_async_copy(src.at[u * NMA + me], dst.at[u * NMA + me], rsem.at[u]).start()
        lax.fori_loop(1, NMA, one, 0)

    def wait_bytes(ref, sem):
        pltpu.make_async_copy(ref, ref, sem).wait()

    for u in range(2):
        all_to_all(sendbuf, recvbuf, f_send, f_recv, u)

    for b in range(4):
        blk = slice(256 * b, 256 * b + 256)
        perm[blk, :] = onehot(keyr_ref[...] == iota((256, 1024), 0) + 256 * b)
        permt[blk, :] = onehot(keyc_ref[blk] == iota((256, 1024), 1))

    tab_f.wait()
    tab_i.wait()

    def near_of(lane_id, u):
        l12 = jnp.where(lane_id >= 116, lane_id - 116, lax.rem(lane_id, 12))
        h = l12 >= 6
        v = jnp.where(h, l12 - 6, l12)
        j = 128 * v + 64 * u + me
        return jnp.where(h, 768 - j, j + 1)

    scale = NPHI ** (-0.5)

    for u in range(2):
        wait_bytes(recvbuf.at[pl.ds(u * NMA, NMA)], f_recv.at[u])
        got = recvbuf[u * NMA : (u + 1) * NMA].reshape(1024, 128)
        lane2 = lax.rem(iota((256, 256), 1), 128)
        near2 = near_of(lane2, u)
        for b in range(4):
            blk = slice(256 * b, 256 * b + 256)
            r = iota((256, 256), 0) + 256 * (b % 2)
            own_live = 3 * r <= 2 * near2
            far_live = 3 * r <= 2 * (769 - near2)
            odd_live = 3 * ((M - 1) - 2 * r) <= 4 * near2
            sorted_blk = dot(perm[blk, :], got).astype(BF16)
            wide = dot(sorted_blk, exp_ref[...])
            rhs_e[blk, :] = jnp.where(own_live, wide[:, 0:256], 0.0).astype(BF16)
            other = jnp.where(far_live, wide[:, 512:768], wide[:, 256:512])
            rhs_o[blk, :] = jnp.where(odd_live, other, 0.0).astype(BF16)

        def longitudes(i, carry):
            spot = pl.ds(pl.multiple_of(i * PB, PB), PB)
            ve = dot(fwd_tab[0, spot, :], rhs_e[...])
            vo = dot(fwd_tab[1, spot, :], rhs_o[...])
            first = cross(ve + vo)
            second = cross(ve - vo)
            summed[spot, :] = (first + second).astype(BF16)
            differ[spot, :] = (first - second).astype(BF16)
            return carry

        lax.fori_loop(0, HALF // PB, longitudes, 0)

        lane1 = iota((256, 128), 1)
        near1 = near_of(lane1, u)
        main = lane1 < 96
        for b in range(4):
            blk = slice(256 * b, 256 * b + 256)
            r = iota((256, 128), 0) + 256 * (b % 2)
            own_live = (3 * r <= 2 * near1) & main
            both_live = (3 * ((M - 1) - 2 * r) <= 4 * near1) & (3 * r <= 2 * (769 - near1)) & main
            se = dot(inv_tab[0, blk, :], summed[...]) * scale
            so = dot(inv_tab[1, blk, :], differ[...]) * scale
            so = so.astype(BF16)
            rest = jnp.where(both_live, so.astype(F32), 0.0).astype(BF16)
            moved = dot(so, fold_ref[0:128, :]) + dot(rest, fold_ref[128:256, :])
            pout[blk, :] = jnp.where(own_live, se, moved).astype(BF16)
        for b in range(4):
            blk = slice(256 * b, 256 * b + 256)
            outbuf[u * NMA + 16 * b : u * NMA + 16 * b + 16] = (
                dot(permt[blk, :], pout[...]).astype(BF16).reshape(16, 16, 128)
            )
        all_to_all(outbuf, backbuf, b_send, b_recv, u)

    def rad_send(u):
        for step in range(1, NR):
            to = lax.rem(lev + step, NR)
            pltpu.make_async_remote_copy(
                src_ref=backbuf.at[pl.ds(u * NMA + 16 * to, 16)],
                dst_ref=radbuf.at[u, lev],
                send_sem=y_send.at[u],
                recv_sem=y_recv.at[u],
                device_id=(to, me),
                device_id_type=MESH,
            ).start()
        pltpu.make_async_copy(
            backbuf.at[pl.ds(u * NMA + 16 * lev, 16)], radbuf.at[u, lev], y_recv.at[u]
        ).start()

    def rad_derive(u):
        wait_bytes(radbuf.at[u], y_recv.at[u])
        vals = [radbuf[u, k].astype(F32) for k in range(NR)]
        for i in range(NR):
            acc = vals[0] * float(DERIV[i, 0])
            for k in range(1, NR):
                acc = acc + vals[k] * float(DERIV[i, k])
            dersend[u, i] = acc.astype(BF16)
        for step in range(1, NR):
            to = lax.rem(lev + step, NR)
            pltpu.make_async_remote_copy(
                src_ref=dersend.at[u, to],
                dst_ref=derbuf.at[pl.ds(u * NMA + 16 * lev, 16)],
                send_sem=d_send.at[u],
                recv_sem=d_recv.at[u],
                device_id=(to, me),
                device_id_type=MESH,
            ).start()
        pltpu.make_async_copy(
            dersend.at[u, lev], derbuf.at[pl.ds(u * NMA + 16 * lev, 16)], d_recv.at[u]
        ).start()

    def unpack(buf, out_ref):
        turned[...] = buf[...].astype(F32).reshape(2048, 128)
        for row in range(16):
            packed[pl.ds(row, 128, stride=16), :] = turned[pl.ds(row, 128, stride=16), :].T
        for v in range(6):
            live = masks(v)
            for g, grp in enumerate(OUT_GROUPS):
                half = []
                for h in range(2):
                    spot = (grp * 12 + h * 6 + v) * 16
                    half.append(packed[spot : spot + 16, :])
                for h in range(2):
                    spot = (96 + h * 6 + g) * 16
                    rest = packed[spot : spot + 16, :]
                    cols = slice(768 * h + 128 * v, 768 * h + 128 * v + 128)
                    rows[32 * g : 32 * g + 16, cols] = jnp.where(live[h][0], half[h], 0.0).astype(BF16)
                    other = jnp.where(live[1 - h][0], rest, half[1 - h])
                    rows[32 * g + 16 : 32 * g + 32, cols] = jnp.where(live[h][1], other, 0.0).astype(BF16)
        for w in range(6):
            cols = slice(256 * w, 256 * w + 256)
            out_ref[:, cols] = dot(qback[...], rows[:, cols]).astype(BF16)

    wait_bytes(backbuf.at[pl.ds(0, NMA)], b_recv.at[0])
    rad_send(0)
    wait_bytes(backbuf.at[pl.ds(NMA, NMA)], b_recv.at[1])
    rad_send(1)
    rad_derive(0)
    unpack(backbuf, emf_ref)
    rad_derive(1)
    for u in range(2):
        wait_bytes(derbuf.at[pl.ds(u * NMA, NMA)], d_recv.at[u])
    unpack(derbuf, der_ref)

    for u in range(2):
        wait_bytes(sendbuf.at[pl.ds(0, NMA - 1)], f_send.at[u])
        wait_bytes(outbuf.at[pl.ds(0, NMA - 1)], b_send.at[u])
        wait_bytes(backbuf.at[pl.ds(0, 16 * (NR - 1))], y_send.at[u])
        wait_bytes(dersend.at[u, pl.ds(0, NR - 1)], d_send.at[u])


def per_device(velocity, test_fields, order_slots):
    me = lax.axis_index("ma")
    vel = velocity.reshape(3 * 2 * 16, NTH)
    tst = test_fields.reshape(6 * 2 * 16, NTH)
    firsts = order_slots.reshape(NMA, 8, 2)[:, :, 0]
    evens = jnp.where(firsts % 2 == 0, firsts, M - 1 - firsts)
    key = evens[:, None, :] // 2 + (512 * jnp.arange(2, dtype=I32))[None, :, None]
    key = key.reshape(1024)
    own_first = lax.dynamic_slice_in_dim(firsts, me, 1)[0]
    flag = own_first % 2
    own_even = jnp.where(flag == 0, own_first, M - 1 - own_first)
    own = jnp.broadcast_to(own_even[None, :], (2, 8)).reshape(16, 1)
    comp = jnp.arange(6, dtype=I32)[:, None, None, None]
    eo = jnp.arange(2, dtype=I32)[None, :, None, None]
    kk = jnp.arange(2, dtype=I32)[None, None, :, None]
    ii = jnp.arange(8, dtype=I32)[None, None, None, :]
    tgt = (32 * comp + 16 * kk + 2 * ii + jnp.bitwise_xor(eo, flag[None, None, None, :])).reshape(192)
    fwd, inv = phase_tables()
    vm = pl.BlockSpec(memory_space=pltpu.VMEM)
    hbm = pl.BlockSpec(memory_space=pl.ANY)
    dma = pltpu.SemaphoreType.DMA
    emf, der = pl.pallas_call(
        kernel,
        out_shape=[jax.ShapeDtypeStruct((192, NTH), BF16)] * 2,
        in_specs=[vm] * 9 + [hbm] * 2,
        out_specs=[vm] * 2,
        scratch_shapes=[
            pltpu.VMEM((2, HALF, 1024), BF16),
            pltpu.VMEM((2, 1024, HALF), BF16),
            pltpu.VMEM((2048, 128), F32),
            pltpu.VMEM((2048, 128), F32),
            pltpu.VMEM((128, 16, 128), BF16),
            pltpu.VMEM((128, 16, 128), BF16),
            pltpu.VMEM((1024, 1024), BF16),
            pltpu.VMEM((1024, 1024), BF16),
            pltpu.VMEM((1024, 256), BF16),
            pltpu.VMEM((1024, 256), BF16),
            pltpu.VMEM((HALF, 128), BF16),
            pltpu.VMEM((HALF, 128), BF16),
            pltpu.VMEM((1024, 128), BF16),
            pltpu.VMEM((128, 16, 128), BF16),
            pltpu.VMEM((128, 16, 128), BF16),
            pltpu.VMEM((2, NR, 16, 16, 128), BF16),
            pltpu.VMEM((2, NR, 16, 16, 128), BF16),
            pltpu.VMEM((128, 16, 128), BF16),
            pltpu.VMEM((192, 192), BF16),
            pltpu.VMEM((192, 192), BF16),
            pltpu.VMEM((192, NTH), BF16),
        ]
        + [dma((2,))] * 9,
        compiler_params=pltpu.CompilerParams(
            collective_id=0, has_side_effects=True, vmem_limit_bytes=48 << 20
        ),
    )(
        vel, tst, own, tgt.reshape(192, 1), tgt.reshape(1, 192), key.reshape(1024, 1), key.reshape(1, 1024),
        jnp.asarray(expand_table()), jnp.asarray(fold_table()), jnp.asarray(fwd), jnp.asarray(inv),
    )
    shape = (1, 2, 3, 2, 16, NTH)
    return emf.reshape(shape), der.reshape(shape)


def solution(mesh):
    return jax.shard_map(
        per_device,
        mesh=mesh,
        in_specs=(P("rad", None, None, "ma", None), P("rad", None, None, None, "ma", None), P()),
        out_specs=(P("rad", None, None, None, "ma", None), P("rad", None, None, None, "ma", None)),
        check_vma=False,
    )
```

time: 313 us -> 68.3 us (0.22); the launches traced: 307 us -> 68 us
  local copies, waits for them, and re-layouts: 141 us -> 7.27 us
  other arithmetic: 70.5 us -> 0.31 us
  Pallas kernels: 0 us -> 59.7 us
  blocking collectives: 56.6 us -> 0 us
  starting transfers between devices: 23 us -> 0 us
  matrix products: 15.2 us -> 0 us
    unnamed x52 -> x10, local copies, waits for them, and re-layouts: 71 us -> 5.42 us
    pallas_call x0 -> x1, Pallas kernels: none -> 59.7 us  [per_device(): pl.pallas_call(kernel, out_shape=[jax.ShapeDtypeStruct((192, NTH), BF16)]...]
    another operation x16 -> x0, other arithmetic: 59.1 us -> none
    all_to_all x3 -> x0, blocking collectives: 56.6 us -> none  [the longest x1 28.6 us: per_device(): lax.all_to_all(emf_local, 'ma', split_axis=4, concat_axis=5, tiled=True)]
    all_to_all x7 -> x0, local copies, waits for them, and re-layouts: 41.8 us -> none  [the longest x3 17.2 us: per_device(): lax.all_to_all(emf_local, 'ma', split_axis=4, concat_axis=5, tiled=True)]
    all_to_all x2 -> x0, starting transfers between devices: 23 us -> none  [the longest x1 12.2 us: per_device(): lax.all_to_all(vel_live, 'ma', split_axis=4, concat_axis=3, tiled=True)]
    dot_general x19 -> x0, matrix products: 15.2 us -> none  [the longest x6 4.97 us: cycle_emf(): jnp.dot(phase_rows, emf_cycle, preferred_element_type=jnp.float32)]
    reshape x3 -> x2, local copies, waits for them, and re-layouts: 15 us -> 0.96 us  [the longest x1 0.89 us: per_device(): firsts = order_slots.reshape(NMA, 8, 2)[:, :, 0]]
  transfers between devices with their start and end apart: 2 -> 0, of which waited for: 0 -> 0; matrix products, arithmetic and copies ran while one was open for 37% -> 0% of each run, Pallas kernels for 0% -> 0%
where the time goes in v1:
time: 68.3 us; the launch traced here: 68 us
  Pallas kernels  59.7 us (87%)
  local copies, waits for them, and re-layouts  7.27 us (11%)
  between operations  0.75 us (1%)
    pallas_call x1, Pallas kernels, per_device(): pl.pallas_call(kernel, out_shape=[jax.ShapeDtypeStruct((192, NTH), BF16)]...  59.7 us
    unnamed x10, local copies, waits for them, and re-layouts  5.42 us

profile of v1, /device:TPU:6, one launch (start us, length us, event | category | flops | bytes accessed | tf_op | source)
XLA Modules:
  0.0 68.0 jit_solution(15737893605236300035)
XLA Ops:
  0.7 0.1 broadcast_add_fusion.3
  0.7 0.1 broadcast_add_fusion.2
  0.8 0.9 %reshape.311 = s32[64,8,2]{2,1,0:T(8,128)S(1)} reshape(s32[1024]{0:T(1024)} %param.9) | data formatting | bytes 8192 | tf_op jit(solution)/shard_map/reshape | solution.py:351
  1.7 0.1 dynamic-slice_reduce_fusion
  1.8 0.1 copy.13
  2.1 0.1 add.147.tgtr_ref
  2.2 0.1 reshape.315.own_ref
  2.2 0.1 copy.14
  2.3 0.1 broadcast_add_fusion
  2.4 0.1 add.153.keyr_ref
  2.6 0.1 add.154.tgtc_ref
  2.7 0.2 add.155.keyc_ref
  2.9 0.0 copy-start
  2.9 1.1 %copy-done = bf16[1,2,3,2,16,1536]{5,4,3,2,1,0:T(8,128)(2,1)S(1)} copy-done((bf16[1,2,3,2,16,1536]{5,4,3,2,1,0:T(8,128)(2,1)S(1)}, bf16[1,2,3,2,16,1536]{5,4,3,2,1,0:T(8,128)(2,1)}, u32[]{:S(2)}) %copy-start) | copy-done | bytes 589848
  4.0 0.0 copy-start.1
  4.0 1.0 %copy-done.1 = bf16[1,3,2,16,1536]{4,3,2,1,0:T(8,128)(2,1)S(1)} copy-done((bf16[1,3,2,16,1536]{4,3,2,1,0:T(8,128)(2,1)S(1)}, bf16[1,3,2,16,1536]{4,3,2,1,0:T(8,128)(2,1)}, u32[]{:S(2)}) %copy-start.1) | copy-done | bytes 294936
  4.9 0.0 copy-start.2
  4.9 0.9 %copy-done.2 = bf16[128,768]{1,0:T(8,128)(2,1)S(1)} copy-done((bf16[128,768]{1,0:T(8,128)(2,1)S(1)}, bf16[128,768]{1,0:T(8,128)(2,1)}, u32[]{:S(2)}) %copy-start.2) | copy-done | bytes 196632
  5.8 0.0 copy-start.3
  5.9 0.8 %copy-done.3 = bf16[256,128]{1,0:T(8,128)(2,1)S(1)} copy-done((bf16[256,128]{1,0:T(8,128)(2,1)S(1)}, bf16[256,128]{1,0:T(8,128)(2,1)}, u32[]{:S(2)}) %copy-start.3) | copy-done | bytes 65560
  6.7 59.7 %shard_map.86 = (bf16[192,1536]{1,0:T(8,128)(2,1)S(1)}, bf16[192,1536]{1,0:T(8,128)(2,1)S(1)}) custom-call(bf16[96,1536]{1,0:T(8,128)(2,1)S(1)} %bitcast.19, bf16[192,1536]{1,0:T(8,128)(2,1)S(1)} %bitcast.18, s32[16,1]{1,0:T(8,128)S(1)} %reshape.315.own_ref, s32[192,1]{1,0:T(8,128)S(1)} %add.154.tgtc_ref, s32[1,192]{1,0:T(1,128)S(1)} %add.147.tgtr_ref, ...), custom_call_target="tpu_custom_call" | custom-call | tf_op jit(solution)/shard_map/pallas_call | solution.py:368
  66.4 0.8 %copy.20 = bf16[1,2,3,2,16,1536]{5,4,3,2,1,0:T(8,128)(2,1)} copy(bf16[1,2,3,2,16,1536]{5,4,3,2,1,0:T(8,128)(2,1)S(1)} %bitcast.17) | data formatting | bytes 1179648
  67.2 0.8 %copy.21 = bf16[1,2,3,2,16,1536]{5,4,3,2,1,0:T(8,128)(2,1)} copy(bf16[1,2,3,2,16,1536]{5,4,3,2,1,0:T(8,128)(2,1)S(1)} %bitcast.16) | data formatting | bytes 1179648
  (9 shorter events, 0.1 us)
Async XLA Ops:
  2.9 1.1 %copy-start = (bf16[1,2,3,2,16,1536]{5,4,3,2,1,0:T(8,128)(2,1)S(1)}, bf16[1,2,3,2,16,1536]{5,4,3,2,1,0:T(8,128)(2,1)}, u32[]{:S(2)}) copy-start(bf16[1,2,3,2,16,1536]{5,4,3,2,1,0:T(8,128)(2,1)} %param.8) | copy-start | bytes 1769476
  4.0 1.0 %copy-start.1 = (bf16[1,3,2,16,1536]{4,3,2,1,0:T(8,128)(2,1)S(1)}, bf16[1,3,2,16,1536]{4,3,2,1,0:T(8,128)(2,1)}, u32[]{:S(2)}) copy-start(bf16[1,3,2,16,1536]{4,3,2,1,0:T(8,128)(2,1)} %param.7) | copy-start | bytes 884740
  4.9 0.9 %copy-start.2 = (bf16[128,768]{1,0:T(8,128)(2,1)S(1)}, bf16[128,768]{1,0:T(8,128)(2,1)}, u32[]{:S(2)}) copy-start(bf16[128,768]{1,0:T(8,128)(2,1)} %constant.64.clone.exp_ref) | copy-start | bytes 589828
  5.8 0.8 %copy-start.3 = (bf16[256,128]{1,0:T(8,128)(2,1)S(1)}, bf16[256,128]{1,0:T(8,128)(2,1)}, u32[]{:S(2)}) copy-start(bf16[256,128]{1,0:T(8,128)(2,1)} %constant.65.clone.fold_ref) | copy-start | bytes 196612

commit v2 on v1

v2 whole, which is shorter than its diff:
```python
import functools

import jax
import jax.numpy as jnp
import numpy as np
from jax import lax
from jax.experimental import pallas as pl
from jax.experimental.pallas import tpu as pltpu
from jax.sharding import PartitionSpec as P

MESH = pl.DeviceIdType.MESH
M = 1024
NTH = 1536
NPHI = 3072
QUART = NPHI // 4
PAIRS = M // 2
NR = 4
NMA = 64
F32 = jnp.float32
BF16 = jnp.bfloat16
I32 = jnp.int32
PB = 256
EMF_HOME = (False, True)


def cheb_matrix(level_count):
    levels_at = np.arange(level_count)
    points = np.cos(np.pi * levels_at / (level_count - 1))
    weights = np.where((levels_at == 0) | (levels_at == level_count - 1), 2.0, 1.0) * np.where(
        levels_at % 2 == 0, 1.0, -1.0
    )
    identity = np.eye(level_count)
    spread = points[:, None] - points[None, :] + identity
    offdiag = weights[:, None] / weights[None, :] / spread * (1.0 - identity)
    matrix = offdiag - identity * offdiag.sum(axis=1)[:, None]
    return np.asarray(matrix / level_count, dtype=np.float32)


DERIV = cheb_matrix(NR)


def phase_tables():
    r = np.arange(M // 2)
    p = np.arange(QUART + 1)
    fwd = np.zeros((2, 2, QUART + 16, M // 2), np.float32)
    inv = np.zeros((2, 2, M // 2, QUART), np.float32)
    for par, m in enumerate((2 * r, M - 1 - 2 * r)):
        q = (p[:, None] * m[None, :]) % NPHI
        ang = q.astype(np.float32) * np.float32(2.0 * np.pi / NPHI)
        for k, tab in enumerate((np.cos(ang), -np.sin(ang))):
            fwd[par, k, : QUART + 1] = tab
            inv[par, k] = tab[:QUART].T
    inv[:, :, :, 0] *= 0.5
    sign = np.where(r % 2 == 0, 1.0, -1.0)
    fwd[:, :, QUART] = 0.0
    fwd[0, 0, QUART] = sign
    fwd[1, 1, QUART] = sign
    return fwd.astype(jnp.bfloat16), inv.astype(jnp.bfloat16)


def expand_table():
    tab = np.zeros((3, 128, 256), np.float32)
    groups = []
    for f in range(2):
        for g, c in enumerate((1, 2, 0, 1)):
            groups.append((12 * (4 * f + g), c))
    b_first = 128 + 116
    for f in range(2):
        base = 3 + 3 * f
        for g, c in enumerate((2, 0, 1)):
            groups.append((128 + 12 * (4 * f + g), base + c))
        groups.append((b_first if f == 0 else 128 + 36, base + 1))
    for lane0, c in groups:
        for h in range(2):
            for v in range(6):
                lane = lane0 + h * 6 + v
                tab[0, c * 12 + h * 6 + v, lane] = 1
                tab[1, c * 12 + (1 - h) * 6 + v, lane] = 1
                tab[2, 108 + h * 9 + c, lane] = 1
    return np.concatenate(list(tab), axis=1).astype(jnp.bfloat16)


OUT_GROUPS = (0, 1, 2, 4, 5, 6)


def fold_table():
    tab = np.zeros((2, 128, 128), np.float32)
    for g, grp in enumerate(OUT_GROUPS):
        for h in range(2):
            for v in range(6):
                lane = grp * 12 + h * 6 + v
                tab[0, grp * 12 + (1 - h) * 6 + v, lane] = 1
                tab[1, lane, 96 + h * 6 + g] = 1
    return np.concatenate(list(tab), axis=0).astype(jnp.bfloat16)


def dot(a, b):
    return jnp.dot(a, b, preferred_element_type=F32)


def iota(shape, dim):
    return lax.broadcasted_iota(I32, shape, dim)


def onehot(cond):
    return jnp.where(cond, 1.0, 0.0).astype(BF16)


def cross(x):
    a, b = x[:, :128], x[:, 128:]
    return a * b - pltpu.roll(a, 116, 1) * pltpu.roll(b, 12, 1)


def kernel(
    slot_smem, slot_ref, vel_hbm, tst_hbm, exp_hbm, fold_hbm, fwd_hbm, inv_hbm,
    emf_ref, der_ref,
    vel_ref, tst_ref, exp_ref, fold_ref, fwd_raw, inv_raw, fwd_tab, inv_tab, packed, turned, sendbuf, recvbuf,
    perm, permt, triple, sign, rhs, folded, outbuf, backbuf, radbuf, dersend, derbuf, quse, qback, rows,
    load_sem, f_send, f_recv, b_send, b_recv, y_send, y_recv, d_send, d_recv, own_send, e_send, ready,
):
    me = lax.axis_index("ma")
    lev = lax.axis_index("rad")

    barrier = pltpu.get_barrier_semaphore()

    def greet(step, carry):
        pl.semaphore_signal(
            barrier, inc=1, device_id=(lev, lax.rem(me + step, NMA)), device_id_type=MESH
        )
        return carry

    loads = [
        pltpu.make_async_copy(src, dst, load_sem.at[i])
        for i, (src, dst) in enumerate(
            (
                (vel_hbm, vel_ref), (tst_hbm, tst_ref), (fwd_hbm, fwd_raw), (inv_hbm, inv_raw),
                (exp_hbm, exp_ref), (fold_hbm, fold_ref),
            )
        )
    ]
    loads[0].start()
    loads[1].start()
    lax.fori_loop(1, NMA, greet, 0)
    for step in range(1, NR):
        pl.semaphore_signal(barrier, inc=1, device_id=(lax.rem(lev + step, NR), me), device_id_type=MESH)
    for load in loads[2:]:
        load.start()

    firsts = [slot_smem[me * 16 + 2 * i] for i in range(8)]

    def spread(pair, shape):
        out = jnp.full(shape, firsts[7], I32)
        for i in range(7):
            out = jnp.where(pair == i, firsts[i], out)
        return out

    def onehot_rows(dim):
        here = iota((192, 192), dim)
        first = spread(here & 7, (192, 192))
        slot = (here & ~31) + ((here & 8) << 1) + 2 * (here & 7) + (((here >> 4) ^ first) & 1)
        return onehot(slot == iota((192, 192), 1 - dim))

    quse[...] = onehot_rows(0)
    qback[...] = onehot_rows(1)
    lane = iota((16, 128), 1)
    first = spread(iota((16, 128), 0) & 7, (16, 128))
    even = jnp.where((first & 1) == 0, first, (M - 1) - first)
    odd = (M - 1) - even

    def masks(v):
        out = []
        for h in range(2):
            j = 128 * v + lane
            near = (j + 1) if h == 0 else (768 - j)
            out.append((even * NTH <= 2 * M * near, odd * NTH <= 2 * M * near))
        return out

    loads[0].wait()
    loads[1].wait()
    left = {}
    for w in range(3):
        halves = []
        for h in range(2):
            cols = slice(768 * h + 256 * w, 768 * h + 256 * w + 256)
            halves.append(
                (dot(quse[0:96, 0:96], vel_ref[:, cols]), dot(quse[...], tst_ref[:, cols]))
            )
        for vv in range(2):
            v = 2 * w + vv
            live = masks(v)
            for c in range(9):
                xe, xo = [], []
                for h in range(2):
                    src = halves[h][0] if c < 3 else halves[h][1]
                    row = 32 * (c if c < 3 else c - 3)
                    xe.append(src[row : row + 16, 128 * vv : 128 * vv + 128])
                    xo.append(src[row + 16 : row + 32, 128 * vv : 128 * vv + 128])
                for h in range(2):
                    spot = (c * 12 + h * 6 + v) * 16
                    packed[spot : spot + 16, :] = jnp.where(live[h][0], xe[h], xo[1 - h])
                    rest = jnp.where(live[h][1] & live[1 - h][0], xo[h], 0.0)
                    left[h, c] = rest if v == 0 else left[h, c] + rest
    for h in range(2):
        for c in range(9):
            spot = (108 + h * 9 + c) * 16
            packed[spot : spot + 16, :] = left[h, c]
    packed[126 * 16 : 128 * 16, :] = jnp.zeros((32, 128), F32)
    for row in range(16):
        turned[pl.ds(row, 128, stride=16), :] = packed[pl.ds(row, 128, stride=16), :].T
    sendbuf[...] = turned[...].astype(BF16).reshape(128, 16, 128)

    pl.semaphore_wait(barrier, NMA - 1 + NR - 1)
    for step in range(1, NR):
        pl.semaphore_signal(ready, inc=1, device_id=(lax.rem(lev + step, NR), me), device_id_type=MESH)

    def all_to_all(src, dst, ssem, rsem, u):
        def one(step, carry):
            to = lax.rem(me + step, NMA)
            pltpu.make_async_remote_copy(
                src_ref=src.at[u * NMA + to],
                dst_ref=dst.at[u * NMA + me],
                send_sem=ssem.at[u],
                recv_sem=rsem.at[u],
                device_id=(lev, to),
                device_id_type=MESH,
            ).start()
            return carry

        pltpu.make_async_copy(src.at[u * NMA + me], dst.at[u * NMA + me], rsem.at[u]).start()
        lax.fori_loop(1, NMA, one, 0)

    deriver = me // 16
    place = lax.rem(me, 16)

    def to_deriver(u):
        def one(step, carry):
            to = lax.rem(me + step, NMA)
            pltpu.make_async_remote_copy(
                src_ref=outbuf.at[u * NMA + to],
                dst_ref=radbuf.at[u, lev, place],
                send_sem=y_send.at[u],
                recv_sem=y_recv.at[u],
                device_id=(deriver, to),
                device_id_type=MESH,
            ).start()
            return carry

        lax.fori_loop(1, NMA, one, 0)

        @pl.when(deriver == lev)
        def _():
            pltpu.make_async_copy(outbuf.at[u * NMA + me], radbuf.at[u, lev, place], y_recv.at[u]).start()

        @pl.when(deriver != lev)
        def _():
            pltpu.make_async_remote_copy(
                src_ref=outbuf.at[u * NMA + me],
                dst_ref=radbuf.at[u, lev, place],
                send_sem=own_send.at[u],
                recv_sem=y_recv.at[u],
                device_id=(deriver, me),
                device_id_type=MESH,
            ).start()

    def wait_bytes(ref, sem):
        pltpu.make_async_copy(ref, ref, sem).wait()

    for u in range(2):
        all_to_all(sendbuf, recvbuf, f_send, f_recv, u)

    slots = slot_ref[...]
    rank = jnp.where((slots & 1) == 0, slots, (M - 1) - slots) >> 1
    high = (rank >> 4).astype(F32).astype(BF16)
    low = (rank & 15).astype(F32).astype(BF16)
    at_row, at_lane = iota((128, 128), 0), iota((128, 128), 1)
    parts = []
    for side in range(2):
        pick = onehot(at_row == 2 * (at_lane - 64 * side))
        parts.append(dot(high, pick) * 16.0 + dot(low, pick))
    keys = jnp.concatenate([parts[0][2 * b : 2 * b + 1] + parts[1][2 * b + 1 : 2 * b + 2] for b in range(4)] * 2, axis=0)
    keys_t = keys.T
    for b in range(4):
        blk = slice(128 * b, 128 * b + 128)
        perm[:, blk] = onehot(keys[b : b + 1, :] == iota((PAIRS, 128), 0).astype(F32))
        column = keys_t[:, b : b + 1]
        permt[blk, :] = onehot(column == iota((128, PAIRS), 1).astype(F32))
        wide = jnp.broadcast_to(column, (128, 128)).astype(I32)
        triple[blk, :] = 3 * wide
        sign[blk, :] = (1 - 2 * (wide & 1)).astype(F32)

    for load in loads[2:]:
        load.wait()

    def build(i, carry):
        for par in range(2):
            for k in range(2):
                spot = pl.ds(pl.multiple_of(i * 256, 256), 256)
                fwd_tab[par, k, spot, :] = dot(fwd_raw[par, k, spot, :], perm[...]).astype(BF16)
                inv_tab[par, k, :, spot] = dot(permt[...], inv_raw[par, k, :, spot]).astype(BF16)
        return carry

    lax.fori_loop(0, QUART // 256, build, 0)
    for par in range(2):
        for k in range(2):
            last = slice(QUART, QUART + 16)
            fwd_tab[par, k, last, :] = dot(fwd_raw[par, k, last, :], perm[...]).astype(BF16)

    def near_of(lane_id, u):
        l12 = jnp.where(lane_id >= 116, lane_id - 116, lax.rem(lane_id, 12))
        h = l12 >= 6
        v = jnp.where(h, l12 - 6, l12)
        j = 128 * v + 64 * u + me
        return jnp.where(h, 768 - j, j + 1)

    scale = NPHI ** (-0.5)

    for u in range(2):
        lane1 = iota((1, 128), 1)
        near = near_of(lane1, u)
        main = lane1 < 96
        own_top, far_top, odd_low = 2 * near, 1538 - 2 * near, 1535 - 2 * near
        wait_bytes(recvbuf.at[pl.ds(u * NMA, NMA)], f_recv.at[u])
        for b in range(4):
            blk = slice(128 * b, 128 * b + 128)
            got = recvbuf[u * NMA + 16 * b : u * NMA + 16 * b + 16].reshape(256, 128)
            wide = dot(got, exp_ref[...]).reshape(16, 2, 8, 768)
            tri = triple[blk, :]
            own_live = tri <= own_top
            far_live = tri <= far_top
            odd_live = tri >= odd_low
            for k in range(2):
                part = wide[:, k].reshape(128, 768)
                for t in range(2):
                    cols = slice(128 * t, 128 * t + 128)
                    same, swap, rest = (part[:, 256 * i + 128 * t : 256 * i + 128 * t + 128] for i in range(3))
                    rhs[0, k, blk, cols] = jnp.where(own_live, same, 0.0).astype(BF16)
                    other = jnp.where(far_live, rest, swap)
                    rhs[1, k, blk, cols] = jnp.where(odd_live, other, 0.0).astype(BF16)

        def longitudes(i, carry):
            spot = pl.ds(pl.multiple_of(i * PB, PB), PB)
            ce, se, co, so = (
                dot(fwd_tab[par, k, spot, :], rhs[par, k]) for par in range(2) for k in range(2)
            )
            ve, vo = ce + se, co + so
            me_, mo = ce - se, so - co
            e1, e2 = cross(ve + vo), cross(ve - vo)
            e3, e4 = cross(me_ + mo), cross(me_ - mo)
            us, ws, um, wm = e1 + e2, e1 - e2, e3 + e4, e3 - e4
            folded[0, 0, spot, :] = (us + um).astype(BF16)
            folded[0, 1, spot, :] = (us - um).astype(BF16)
            folded[1, 0, spot, :] = (ws - wm).astype(BF16)
            folded[1, 1, spot, :] = (ws + wm).astype(BF16)
            return carry

        lax.fori_loop(0, QUART // PB, longitudes, 0, unroll=True)
        last = slice(QUART, QUART + 16)
        ve, vo = (
            dot(fwd_tab[par, 0, last, :], rhs[par, 0]) + dot(fwd_tab[par, 1, last, :], rhs[par, 1])
            for par in range(2)
        )
        e1, e2 = cross(ve + vo), cross(ve - vo)
        quarter = ((e1 + e2)[0:1], (e1 - e2)[0:1])

        for b in range(2):
            blk = slice(256 * b, 256 * b + 256)
            tri = triple[blk, :]
            own_live = (tri <= own_top) & main
            both_live = (tri >= odd_low) & (tri <= far_top) & main
            out = []
            for k in range(2):
                se = dot(inv_tab[0, k, blk, :], folded[0, k])
                so = dot(inv_tab[1, k, blk, :], folded[1, k])
                if k == 0:
                    se = se + sign[blk, :] * quarter[0]
                else:
                    so = so + sign[blk, :] * quarter[1]
                so = so * scale
                rest = jnp.where(both_live, so, 0.0)
                moved = dot(jnp.concatenate([so, rest], axis=1).astype(BF16), fold_ref[...])
                out.append(jnp.where(own_live, se * scale, moved).reshape(32, 1, 8, 128))
            outbuf[u * NMA + 32 * b : u * NMA + 32 * b + 32] = (
                jnp.concatenate(out, axis=1).reshape(32, 16, 128).astype(BF16)
            )
        if u == 0:
            pl.semaphore_wait(ready, NR - 1)
        to_deriver(u)
        if EMF_HOME[u]:
            all_to_all(outbuf, backbuf, b_send, b_recv, u)

    def rad_derive(u):
        wait_bytes(radbuf.at[u], y_recv.at[u])
        vals = [radbuf[u, k].astype(F32) for k in range(NR)]
        for i in range(NR):
            acc = vals[0] * float(DERIV[i, 0])
            for k in range(1, NR):
                acc = acc + vals[k] * float(DERIV[i, k])
            dersend[u, i] = acc.astype(BF16)
        for step in range(1, NR):
            to = lax.rem(lev + step, NR)
            pltpu.make_async_remote_copy(
                src_ref=dersend.at[u, to],
                dst_ref=derbuf.at[pl.ds(u * NMA + 16 * lev, 16)],
                send_sem=d_send.at[u],
                recv_sem=d_recv.at[u],
                device_id=(to, me),
                device_id_type=MESH,
            ).start()
        pltpu.make_async_copy(
            dersend.at[u, lev], derbuf.at[pl.ds(u * NMA + 16 * lev, 16)], d_recv.at[u]
        ).start()
        if not EMF_HOME[u]:
            for step in range(1, NR):
                to = lax.rem(lev + step, NR)
                pltpu.make_async_remote_copy(
                    src_ref=radbuf.at[u, to],
                    dst_ref=backbuf.at[pl.ds(u * NMA + 16 * lev, 16)],
                    send_sem=e_send.at[u],
                    recv_sem=b_recv.at[u],
                    device_id=(to, me),
                    device_id_type=MESH,
                ).start()
            pltpu.make_async_copy(
                radbuf.at[u, lev], backbuf.at[pl.ds(u * NMA + 16 * lev, 16)], b_recv.at[u]
            ).start()

    def unpack(buf, out_ref):
        turned[...] = buf[...].astype(F32).reshape(2048, 128)
        for row in range(16):
            packed[pl.ds(row, 128, stride=16), :] = turned[pl.ds(row, 128, stride=16), :].T
        for v in range(6):
            live = masks(v)
            for g, grp in enumerate(OUT_GROUPS):
                half = []
                for h in range(2):
                    spot = (grp * 12 + h * 6 + v) * 16
                    half.append(packed[spot : spot + 16, :])
                for h in range(2):
                    spot = (96 + h * 6 + g) * 16
                    rest = packed[spot : spot + 16, :]
                    cols = slice(768 * h + 128 * v, 768 * h + 128 * v + 128)
                    rows[32 * g : 32 * g + 16, cols] = jnp.where(live[h][0], half[h], 0.0).astype(BF16)
                    other = jnp.where(live[1 - h][0], rest, half[1 - h])
                    rows[32 * g + 16 : 32 * g + 32, cols] = jnp.where(live[h][1], other, 0.0).astype(BF16)
        for w in range(6):
            cols = slice(256 * w, 256 * w + 256)
            out_ref[:, cols] = dot(qback[...], rows[:, cols]).astype(BF16)

    for u in range(2):
        rad_derive(u)
    for u in range(2):
        wait_bytes(backbuf.at[pl.ds(u * NMA, NMA)], b_recv.at[u])
    unpack(backbuf, emf_ref)
    for u in range(2):
        wait_bytes(derbuf.at[pl.ds(u * NMA, NMA)], d_recv.at[u])
    unpack(derbuf, der_ref)

    for u in range(2):
        wait_bytes(sendbuf.at[pl.ds(0, NMA - 1)], f_send.at[u])
        wait_bytes(outbuf.at[pl.ds(0, NMA - 1)], y_send.at[u])

        @pl.when(deriver != lev)
        def _():
            wait_bytes(outbuf.at[0], own_send.at[u])

        wait_bytes(dersend.at[u, pl.ds(0, NR - 1)], d_send.at[u])
        if EMF_HOME[u]:
            wait_bytes(outbuf.at[pl.ds(0, NMA - 1)], b_send.at[u])
        else:
            wait_bytes(radbuf.at[u, pl.ds(0, NR - 1)], e_send.at[u])


def per_device(velocity, test_fields, order_slots):
    vel = velocity.reshape(3 * 2 * 16, NTH)
    tst = test_fields.reshape(6 * 2 * 16, NTH)
    fwd, inv = phase_tables()
    vm = pl.BlockSpec(memory_space=pltpu.VMEM)
    sm = pl.BlockSpec(memory_space=pltpu.SMEM)
    hbm = pl.BlockSpec(memory_space=pl.ANY)
    dma = pltpu.SemaphoreType.DMA

    def vmem(*shape, dtype=BF16):
        return pltpu.VMEM(shape, dtype)

    emf, der = pl.pallas_call(
        kernel,
        out_shape=[jax.ShapeDtypeStruct((192, NTH), BF16)] * 2,
        in_specs=[sm, vm] + [hbm] * 6,
        out_specs=[vm] * 2,
        scratch_shapes=[
            vmem(96, NTH),
            vmem(192, NTH),
            vmem(128, 768),
            vmem(256, 128),
            vmem(2, 2, QUART + 16, PAIRS),
            vmem(2, 2, PAIRS, QUART),
            vmem(2, 2, QUART + 16, PAIRS),
            vmem(2, 2, PAIRS, QUART),
            vmem(2048, 128, dtype=F32),
            vmem(2048, 128, dtype=F32),
            vmem(128, 16, 128),
            vmem(128, 16, 128),
            vmem(PAIRS, PAIRS),
            vmem(PAIRS, PAIRS),
            vmem(PAIRS, 128, dtype=I32),
            vmem(PAIRS, 128, dtype=F32),
            vmem(2, 2, PAIRS, 256),
            vmem(2, 2, QUART, 128),
            vmem(128, 16, 128),
            vmem(128, 16, 128),
            vmem(2, NR, 16, 16, 128),
            vmem(2, NR, 16, 16, 128),
            vmem(128, 16, 128),
            vmem(192, 192),
            vmem(192, 192),
            vmem(192, NTH),
            dma((6,)),
        ]
        + [dma((2,))] * 10
        + [pltpu.SemaphoreType.REGULAR],
        compiler_params=pltpu.CompilerParams(
            collective_id=0, has_side_effects=True, vmem_limit_bytes=60 << 20
        ),
    )(
        order_slots, order_slots.reshape(8, 128), vel, tst,
        jnp.asarray(expand_table()), jnp.asarray(fold_table()), jnp.asarray(fwd), jnp.asarray(inv),
    )
    shape = (1, 2, 3, 2, 16, NTH)
    return emf.reshape(shape), der.reshape(shape)


def solution(mesh):
    return jax.shard_map(
        per_device,
        mesh=mesh,
        in_specs=(P("rad", None, None, "ma", None), P("rad", None, None, None, "ma", None), P()),
        out_specs=(P("rad", None, None, None, "ma", None), P("rad", None, None, None, "ma", None)),
        check_vma=False,
    )
```

time: 68.3 us -> 55 us (0.81)
  the two profiles are of different devices: /device:TPU:6 before, /device:TPU:1 now
where the time goes in v2:
time: 55 us; the launch traced here: 54.7 us
  Pallas kernels  50.3 us (91%)
  local copies, waits for them, and re-layouts  3.83 us (7%)
  between operations  0.64 us (1%)
    pallas_call x1, Pallas kernels, per_device(): pl.pallas_call(kernel, out_shape=[jax.ShapeDtypeStruct((192, NTH), BF16)]...  50.3 us
    unnamed x2, local copies, waits for them, and re-layouts  3.83 us

profile of v2, /device:TPU:1, one launch (start us, length us, event | category | flops | bytes accessed | tf_op | source)
XLA Modules:
  0.0 54.7 jit_solution(10962043462770537539)
XLA Ops:
  0.6 50.3 %shard_map.86 = (bf16[192,1536]{1,0:T(8,128)(2,1)}, bf16[192,1536]{1,0:T(8,128)(2,1)}) custom-call(s32[1024]{0:T(1024)} %slot_smem.1, s32[8,128]{1,0:T(8,128)} %bitcast.9, bf16[96,1536]{1,0:T(8,128)(2,1)} %bitcast.8, bf16[192,1536]{1,0:T(8,128)(2,1)} %bitcast.5, bf16[128,768]{1,0:T(8,128)(2,1)} %constant.8.clone.exp_hbm, ...), custom_call_target="tpu_custom_call" | custom-call | tf_op jit(solution)/shard_map/pallas_call | solution.py:485
  50.9 1.9 %copy.11 = bf16[1,2,3,2,16,1536]{5,4,3,2,1,0:T(8,128)(2,1)} copy(bf16[1,2,3,2,16,1536]{5,4,3,2,1,0:T(8,128)(2,1)} %bitcast.7) | data formatting | bytes 1179648
  52.8 1.9 %copy.12 = bf16[1,2,3,2,16,1536]{5,4,3,2,1,0:T(8,128)(2,1)} copy(bf16[1,2,3,2,16,1536]{5,4,3,2,1,0:T(8,128)(2,1)} %bitcast.6) | data formatting | bytes 1179648

commit v3 on v2

--- a/solution.py
+++ b/solution.py
@@ -468,6 +468,18 @@
             wait_bytes(outbuf.at[pl.ds(0, NMA - 1)], b_send.at[u])
         else:
             wait_bytes(radbuf.at[u, pl.ds(0, NR - 1)], e_send.at[u])
+
+
+def settle(emf_in, der_in, emf_out, der_out, sem):
+    copies = []
+    for i, (a, b) in enumerate(((emf_in, emf_out), (der_in, der_out))):
+        for part in range(6):
+            blk = pl.ds(part * (192 // 6), 192 // 6)
+            copies.append(pltpu.make_async_copy(a.at[blk], b.at[blk], sem.at[i, part]))
+    for copy in copies:
+        copy.start()
+    for copy in copies:
+        copy.wait()
 
 
 def per_device(velocity, test_fields, order_slots):
@@ -525,6 +537,13 @@
         order_slots, order_slots.reshape(8, 128), vel, tst,
         jnp.asarray(expand_table()), jnp.asarray(fold_table()), jnp.asarray(fwd), jnp.asarray(inv),
     )
+    emf, der = pl.pallas_call(
+        settle,
+        out_shape=[jax.ShapeDtypeStruct((192, NTH), BF16)] * 2,
+        in_specs=[vm] * 2,
+        out_specs=[hbm] * 2,
+        scratch_shapes=[dma((2, 6))],
+    )(emf, der)
     shape = (1, 2, 3, 2, 16, NTH)
     return emf.reshape(shape), der.reshape(shape)
 

time: 55 us -> 53.4 us (0.971)
  local copies, waits for them, and re-layouts: 3.83 us -> 0 us
  Pallas kernels: 50.3 us -> 52.6 us
    unnamed x2 -> x0, local copies, waits for them, and re-layouts: 3.83 us -> none
    pallas_call x0 -> x1, Pallas kernels: none -> 2.34 us  [per_device(): pl.pallas_call(settle, out_shape=[jax.ShapeDtypeStruct((192, NTH), BF16)]...]
where the time goes in v3:
time: 53.4 us; the launch traced here: 53.3 us
  Pallas kernels  52.6 us (99%)
  between operations  0.64 us (1%)
    pallas_call x1, Pallas kernels, per_device(): pl.pallas_call(kernel, out_shape=[jax.ShapeDtypeStruct((192, NTH), BF16)]...  50.3 us
    pallas_call x1, Pallas kernels, per_device(): pl.pallas_call(settle, out_shape=[jax.ShapeDtypeStruct((192, NTH), BF16)]...  2.34 us

profile of v3, /device:TPU:1, one launch (start us, length us, event | category | flops | bytes accessed | tf_op | source)
XLA Modules:
  0.0 53.3 jit_solution(686775516470368169)
XLA Ops:
  0.6 50.3 %shard_map.86 = (bf16[192,1536]{1,0:T(8,128)(2,1)}, bf16[192,1536]{1,0:T(8,128)(2,1)}) custom-call(s32[1024]{0:T(1024)} %slot_smem.1, s32[8,128]{1,0:T(8,128)} %bitcast.7, bf16[96,1536]{1,0:T(8,128)(2,1)} %bitcast.6, bf16[192,1536]{1,0:T(8,128)(2,1)} %bitcast.5, bf16[128,768]{1,0:T(8,128)(2,1)} %constant.8.clone.exp_hbm, ...), custom_call_target="tpu_custom_call" | custom-call | tf_op jit(solution)/shard_map/pallas_call | solution.py:497
  50.9 2.3 %shard_map.87 = (bf16[192,1536]{1,0:T(8,128)(2,1)}, bf16[192,1536]{1,0:T(8,128)(2,1)}) custom-call(bf16[192,1536]{1,0:T(8,128)(2,1)} %get-tuple-element.6.emf_in, bf16[192,1536]{1,0:T(8,128)(2,1)} %get-tuple-element.7.der_in), custom_call_target="tpu_custom_call" | custom-call | tf_op jit(solution)/shard_map/pallas_call | solution.py:540

commit v4 on v2

--- a/solution.py
+++ b/solution.py
@@ -113,10 +113,10 @@
 
 def kernel(
     slot_smem, slot_ref, vel_hbm, tst_hbm, exp_hbm, fold_hbm, fwd_hbm, inv_hbm,
-    emf_ref, der_ref,
-    vel_ref, tst_ref, exp_ref, fold_ref, fwd_raw, inv_raw, fwd_tab, inv_tab, packed, turned, sendbuf, recvbuf,
+    emf_hbm, der_hbm,
+    emf_ref, der_ref, vel_ref, tst_ref, exp_ref, fold_ref, fwd_raw, inv_raw, fwd_tab, inv_tab, packed, turned, sendbuf, recvbuf,
     perm, permt, triple, sign, rhs, folded, outbuf, backbuf, radbuf, dersend, derbuf, quse, qback, rows,
-    load_sem, f_send, f_recv, b_send, b_recv, y_send, y_recv, d_send, d_recv, own_send, e_send, ready,
+    load_sem, f_send, f_recv, b_send, b_recv, y_send, y_recv, d_send, d_recv, own_send, e_send, out_sem, ready,
 ):
     me = lax.axis_index("ma")
     lev = lax.axis_index("rad")
@@ -232,21 +232,26 @@
     deriver = me // 16
     place = lax.rem(me, 16)
 
-    def to_deriver(u):
+    def to_deriver(u, b):
         def one(step, carry):
-            to = lax.rem(me + step, NMA)
-            pltpu.make_async_remote_copy(
-                src_ref=outbuf.at[u * NMA + to],
-                dst_ref=radbuf.at[u, lev, place],
-                send_sem=y_send.at[u],
-                recv_sem=y_recv.at[u],
-                device_id=(deriver, to),
-                device_id_type=MESH,
-            ).start()
+            to = 32 * b + lax.rem(me + step, 32)
+
+            @pl.when(to != me)
+            def _():
+                pltpu.make_async_remote_copy(
+                    src_ref=outbuf.at[u * NMA + to],
+                    dst_ref=radbuf.at[u, lev, place],
+                    send_sem=y_send.at[u],
+                    recv_sem=y_recv.at[u],
+                    device_id=(deriver, to),
+                    device_id_type=MESH,
+                ).start()
+
             return carry
 
-        lax.fori_loop(1, NMA, one, 0)
-
+        lax.fori_loop(0, 32, one, 0)
+
+    def own_to_deriver(u):
         @pl.when(deriver == lev)
         def _():
             pltpu.make_async_copy(outbuf.at[u * NMA + me], radbuf.at[u, lev, place], y_recv.at[u]).start()
@@ -382,9 +387,10 @@
             outbuf[u * NMA + 32 * b : u * NMA + 32 * b + 32] = (
                 jnp.concatenate(out, axis=1).reshape(32, 16, 128).astype(BF16)
             )
-        if u == 0:
-            pl.semaphore_wait(ready, NR - 1)
-        to_deriver(u)
+            if u == 0 and b == 0:
+                pl.semaphore_wait(ready, NR - 1)
+            to_deriver(u, b)
+        own_to_deriver(u)
         if EMF_HOME[u]:
             all_to_all(outbuf, backbuf, b_send, b_recv, u)
 
@@ -424,7 +430,7 @@
                 radbuf.at[u, lev], backbuf.at[pl.ds(u * NMA + 16 * lev, 16)], b_recv.at[u]
             ).start()
 
-    def unpack(buf, out_ref):
+    def unpack(buf, out_ref, out_hbm, sem):
         turned[...] = buf[...].astype(F32).reshape(2048, 128)
         for row in range(16):
             packed[pl.ds(row, 128, stride=16), :] = turned[pl.ds(row, 128, stride=16), :].T
@@ -443,17 +449,18 @@
                     other = jnp.where(live[1 - h][0], rest, half[1 - h])
                     rows[32 * g + 16 : 32 * g + 32, cols] = jnp.where(live[h][1], other, 0.0).astype(BF16)
         for w in range(6):
-            cols = slice(256 * w, 256 * w + 256)
+            cols = pl.ds(256 * w, 256)
             out_ref[:, cols] = dot(qback[...], rows[:, cols]).astype(BF16)
+            pltpu.make_async_copy(out_ref.at[:, cols], out_hbm.at[:, cols], sem).start()
 
     for u in range(2):
         rad_derive(u)
     for u in range(2):
         wait_bytes(backbuf.at[pl.ds(u * NMA, NMA)], b_recv.at[u])
-    unpack(backbuf, emf_ref)
+    unpack(backbuf, emf_ref, emf_hbm, out_sem.at[0])
     for u in range(2):
         wait_bytes(derbuf.at[pl.ds(u * NMA, NMA)], d_recv.at[u])
-    unpack(derbuf, der_ref)
+    unpack(derbuf, der_ref, der_hbm, out_sem.at[1])
 
     for u in range(2):
         wait_bytes(sendbuf.at[pl.ds(0, NMA - 1)], f_send.at[u])
@@ -468,6 +475,24 @@
             wait_bytes(outbuf.at[pl.ds(0, NMA - 1)], b_send.at[u])
         else:
             wait_bytes(radbuf.at[u, pl.ds(0, NR - 1)], e_send.at[u])
+    wait_bytes(emf_ref, out_sem.at[0])
+    wait_bytes(der_ref, out_sem.at[1])
+
+
+def settle(emf_in, der_in, emf_out, der_out, held, in_sem, out_sem):
+    loads, stores = [], []
+    for i, (src, dst) in enumerate(((emf_in, emf_out), (der_in, der_out))):
+        for part in range(3):
+            blk = pl.ds(part * 64, 64)
+            loads.append(pltpu.make_async_copy(src.at[blk], held.at[i, blk], in_sem.at[i, part]))
+            stores.append(pltpu.make_async_copy(held.at[i, blk], dst.at[blk], out_sem.at[i, part]))
+    for load in loads:
+        load.start()
+    for load, store in zip(loads, stores):
+        load.wait()
+        store.start()
+    for store in stores:
+        store.wait()
 
 
 def per_device(velocity, test_fields, order_slots):
@@ -486,8 +511,10 @@
         kernel,
         out_shape=[jax.ShapeDtypeStruct((192, NTH), BF16)] * 2,
         in_specs=[sm, vm] + [hbm] * 6,
-        out_specs=[vm] * 2,
+        out_specs=[hbm] * 2,
         scratch_shapes=[
+            vmem(192, NTH),
+            vmem(192, NTH),
             vmem(96, NTH),
             vmem(192, NTH),
             vmem(128, 768),
@@ -516,7 +543,7 @@
             vmem(192, NTH),
             dma((6,)),
         ]
-        + [dma((2,))] * 10
+        + [dma((2,))] * 11
         + [pltpu.SemaphoreType.REGULAR],
         compiler_params=pltpu.CompilerParams(
             collective_id=0, has_side_effects=True, vmem_limit_bytes=60 << 20
@@ -525,6 +552,13 @@
         order_slots, order_slots.reshape(8, 128), vel, tst,
         jnp.asarray(expand_table()), jnp.asarray(fold_table()), jnp.asarray(fwd), jnp.asarray(inv),
     )
+    emf, der = pl.pallas_call(
+        settle,
+        out_shape=[jax.ShapeDtypeStruct((192, NTH), BF16)] * 2,
+        in_specs=[hbm] * 2,
+        out_specs=[hbm] * 2,
+        scratch_shapes=[vmem(2, 192, NTH), dma((2, 3)), dma((2, 3))],
+    )(emf, der)
     shape = (1, 2, 3, 2, 16, NTH)
     return emf.reshape(shape), der.reshape(shape)
 

time: 55 us -> 52.4 us (0.953)
  the two profiles are of different devices: /device:TPU:1 before, /device:TPU:6 now
where the time goes in v4:
time: 52.4 us; the launch traced here: 51.5 us
  Pallas kernels  50.9 us (97%)
  between operations  0.64 us (1%)
    pallas_call x1, Pallas kernels, per_device(): pl.pallas_call(kernel, out_shape=[jax.ShapeDtypeStruct((192, NTH), BF16)]...  48.8 us
    pallas_call x1, Pallas kernels, per_device(): pl.pallas_call(settle, out_shape=[jax.ShapeDtypeStruct((192, NTH), BF16)]...  2.13 us

profile of v4, /device:TPU:6, one launch (start us, length us, event | category | flops | bytes accessed | tf_op | source)
XLA Modules:
  0.0 51.5 jit_solution(13040228847966670703)
XLA Ops:
  0.6 48.8 %shard_map.86 = (bf16[192,1536]{1,0:T(8,128)(2,1)}, bf16[192,1536]{1,0:T(8,128)(2,1)}) custom-call(s32[1024]{0:T(1024)} %slot_smem.1, s32[8,128]{1,0:T(8,128)} %bitcast.7, bf16[96,1536]{1,0:T(8,128)(2,1)} %bitcast.6, bf16[192,1536]{1,0:T(8,128)(2,1)} %bitcast.5, bf16[128,768]{1,0:T(8,128)(2,1)} %constant.8.clone.exp_hbm, ...), custom_call_target="tpu_custom_call" | custom-call | tf_op jit(solution)/shard_map/pallas_call | solution.py:510
  49.4 2.1 %shard_map.87 = (bf16[192,1536]{1,0:T(8,128)(2,1)}, bf16[192,1536]{1,0:T(8,128)(2,1)}) custom-call(bf16[192,1536]{1,0:T(8,128)(2,1)} %get-tuple-element.6.emf_in, bf16[192,1536]{1,0:T(8,128)(2,1)} %get-tuple-element.7.der_in), custom_call_target="tpu_custom_call" | custom-call | tf_op jit(solution)/shard_map/pallas_call | solution.py:555

commit v5 on v4

--- a/solution.py
+++ b/solution.py
@@ -19,7 +19,7 @@
 F32 = jnp.float32
 BF16 = jnp.bfloat16
 I32 = jnp.int32
-PB = 256
+PB = 384
 EMF_HOME = (False, True)
 
 
@@ -392,7 +392,10 @@
             to_deriver(u, b)
         own_to_deriver(u)
         if EMF_HOME[u]:
-            all_to_all(outbuf, backbuf, b_send, b_recv, u)
+
+            @pl.when(deriver != lev)
+            def _():
+                all_to_all(outbuf, backbuf, b_send, b_recv, u)
 
     def rad_derive(u):
         wait_bytes(radbuf.at[u], y_recv.at[u])
@@ -415,7 +418,11 @@
         pltpu.make_async_copy(
             dersend.at[u, lev], derbuf.at[pl.ds(u * NMA + 16 * lev, 16)], d_recv.at[u]
         ).start()
-        if not EMF_HOME[u]:
+        if EMF_HOME[u]:
+            pltpu.make_async_copy(
+                radbuf.at[u, lev], backbuf.at[pl.ds(u * NMA + 16 * lev, 16)], b_recv.at[u]
+            ).start()
+        else:
             for step in range(1, NR):
                 to = lax.rem(lev + step, NR)
                 pltpu.make_async_remote_copy(
@@ -472,7 +479,11 @@
 
         wait_bytes(dersend.at[u, pl.ds(0, NR - 1)], d_send.at[u])
         if EMF_HOME[u]:
-            wait_bytes(outbuf.at[pl.ds(0, NMA - 1)], b_send.at[u])
+
+            @pl.when(deriver != lev)
+            def _():
+                wait_bytes(outbuf.at[pl.ds(0, NMA - 1)], b_send.at[u])
+
         else:
             wait_bytes(radbuf.at[u, pl.ds(0, NR - 1)], e_send.at[u])
     wait_bytes(emf_ref, out_sem.at[0])

time: 52.4 us -> 52.5 us (level)
  no operation moved by 1% of the time
where the time goes in v5:
time: 52.5 us; the launch traced here: 51.6 us
  Pallas kernels  50.9 us (97%)
  between operations  0.64 us (1%)
    pallas_call x1, Pallas kernels, per_device(): pl.pallas_call(kernel, out_shape=[jax.ShapeDtypeStruct((192, NTH), BF16)]...  48.8 us
    pallas_call x1, Pallas kernels, per_device(): pl.pallas_call(settle, out_shape=[jax.ShapeDtypeStruct((192, NTH), BF16)]...  2.13 us

profile of v5, /device:TPU:6, one launch (start us, length us, event | category | flops | bytes accessed | tf_op | source)
XLA Modules:
  0.0 51.6 jit_solution(11915207073519664186)
XLA Ops:
  0.6 48.8 %shard_map.86 = (bf16[192,1536]{1,0:T(8,128)(2,1)}, bf16[192,1536]{1,0:T(8,128)(2,1)}) custom-call(s32[1024]{0:T(1024)} %slot_smem.1, s32[8,128]{1,0:T(8,128)} %bitcast.7, bf16[96,1536]{1,0:T(8,128)(2,1)} %bitcast.6, bf16[192,1536]{1,0:T(8,128)(2,1)} %bitcast.5, bf16[128,768]{1,0:T(8,128)(2,1)} %constant.8.clone.exp_hbm, ...), custom_call_target="tpu_custom_call" | custom-call | tf_op jit(solution)/shard_map/pallas_call | solution.py:521
  49.4 2.1 %shard_map.87 = (bf16[192,1536]{1,0:T(8,128)(2,1)}, bf16[192,1536]{1,0:T(8,128)(2,1)}) custom-call(bf16[192,1536]{1,0:T(8,128)(2,1)} %get-tuple-element.6.emf_in, bf16[192,1536]{1,0:T(8,128)(2,1)} %get-tuple-element.7.der_in), custom_call_target="tpu_custom_call" | custom-call | tf_op jit(solution)/shard_map/pallas_call | solution.py:566

commit v6 on v4

--- a/solution.py
+++ b/solution.py
@@ -234,7 +234,7 @@
 
     def to_deriver(u, b):
         def one(step, carry):
-            to = 32 * b + lax.rem(me + step, 32)
+            to = 16 * b + lax.rem(me + step, 16)
 
             @pl.when(to != me)
             def _():
@@ -249,7 +249,7 @@
 
             return carry
 
-        lax.fori_loop(0, 32, one, 0)
+        lax.fori_loop(0, 16, one, 0)
 
     def own_to_deriver(u):
         @pl.when(deriver == lev)
@@ -367,8 +367,8 @@
         e1, e2 = cross(ve + vo), cross(ve - vo)
         quarter = ((e1 + e2)[0:1], (e1 - e2)[0:1])
 
-        for b in range(2):
-            blk = slice(256 * b, 256 * b + 256)
+        for b in range(4):
+            blk = slice(128 * b, 128 * b + 128)
             tri = triple[blk, :]
             own_live = (tri <= own_top) & main
             both_live = (tri >= odd_low) & (tri <= far_top) & main
@@ -383,9 +383,9 @@
                 so = so * scale
                 rest = jnp.where(both_live, so, 0.0)
                 moved = dot(jnp.concatenate([so, rest], axis=1).astype(BF16), fold_ref[...])
-                out.append(jnp.where(own_live, se * scale, moved).reshape(32, 1, 8, 128))
-            outbuf[u * NMA + 32 * b : u * NMA + 32 * b + 32] = (
-                jnp.concatenate(out, axis=1).reshape(32, 16, 128).astype(BF16)
+                out.append(jnp.where(own_live, se * scale, moved).reshape(16, 1, 8, 128))
+            outbuf[u * NMA + 16 * b : u * NMA + 16 * b + 16] = (
+                jnp.concatenate(out, axis=1).reshape(16, 16, 128).astype(BF16)
             )
             if u == 0 and b == 0:
                 pl.semaphore_wait(ready, NR - 1)

time: 52.4 us -> 52.9 us (level); the launches traced: 51.5 us -> 52.6 us
  Pallas kernels: 50.9 us -> 51.8 us
    pallas_call x1, Pallas kernels: 48.8 us -> 49.6 us  [per_device(): pl.pallas_call(kernel, out_shape=[jax.ShapeDtypeStruct((192, NTH), BF16)]...]
where the time goes in v6:
time: 52.9 us; the launch traced here: 52.6 us
  Pallas kernels  51.8 us (98%)
  between operations  0.8 us (2%)
    pallas_call x1, Pallas kernels, per_device(): pl.pallas_call(kernel, out_shape=[jax.ShapeDtypeStruct((192, NTH), BF16)]...  49.6 us
    pallas_call x1, Pallas kernels, per_device(): pl.pallas_call(settle, out_shape=[jax.ShapeDtypeStruct((192, NTH), BF16)]...  2.13 us

profile of v6, /device:TPU:6, one launch (start us, length us, event | category | flops | bytes accessed | tf_op | source)
XLA Modules:
  0.0 52.6 jit_solution(7524693358741049067)
XLA Ops:
  0.6 49.6 %shard_map.86 = (bf16[192,1536]{1,0:T(8,128)(2,1)}, bf16[192,1536]{1,0:T(8,128)(2,1)}) custom-call(s32[1024]{0:T(1024)} %slot_smem.1, s32[8,128]{1,0:T(8,128)} %bitcast.7, bf16[96,1536]{1,0:T(8,128)(2,1)} %bitcast.6, bf16[192,1536]{1,0:T(8,128)(2,1)} %bitcast.5, bf16[128,768]{1,0:T(8,128)(2,1)} %constant.8.clone.exp_hbm, ...), custom_call_target="tpu_custom_call" | custom-call | tf_op jit(solution)/shard_map/pallas_call | solution.py:510
  50.3 2.1 %shard_map.87 = (bf16[192,1536]{1,0:T(8,128)(2,1)}, bf16[192,1536]{1,0:T(8,128)(2,1)}) custom-call(bf16[192,1536]{1,0:T(8,128)(2,1)} %get-tuple-element.6.emf_in, bf16[192,1536]{1,0:T(8,128)(2,1)} %get-tuple-element.7.der_in), custom_call_target="tpu_custom_call" | custom-call | tf_op jit(solution)/shard_map/pallas_call | solution.py:555
